TPU v7x, 32 devices: a whole 2x2x4 slice. The times are simulated.
32 devices in a mesh: parts: 2 (over y), tiles: 8 (over z, x), mesh: 2 (over core).
Axes of the slice: x: 2, y: 2, z: 4, core: 2. Of those that a mesh axis runs over, the one named last changes fastest.
Arguments:
- patches: bfloat16 [1024, 128, 128], P(('parts', 'tiles', 'mesh')), parts along dimension 0, may hold values from -6 to 6
- send_index: int32 [32, 32], P(('parts', 'tiles', 'mesh')), parts along dimension 0, may hold values from 0 to 32, as said below
- pair_slots: int32 [32, 2, 16], P(('parts', 'tiles', 'mesh')), parts along dimension 0, may hold values from 0 to 32, as said below
- node_links: int32 [32, 4, 128], P(('parts', 'tiles', 'mesh')), parts along dimension 0, may hold values from 0 to 31
Outputs:
- pair_flow: float32 [2, 512], P(None, ('parts', 'tiles', 'mesh')), parts along dimension 1
- relaxed: float32 [2, 4096], P(None, ('parts', 'tiles', 'mesh')), parts along dimension 1
There are 2 independent parts, one for each index of `parts`. A program takes and returns all parts, laid end to end along the dimension named above; each array names one. Nothing has to cross between parts.
Inputs may be any that keep to these rules, and one draw needn't show every extreme that they name: `send_index`: each patch is sent to at most one owner, as one side of one tile pair; a live pair's two sides come from two different tiles and pair_slots names their received slots, numbered source tile times 4 plus slot; the value 2 * 16 marks an empty send slot. Some device fills all 4 slots to one peer. `pair_slots`: the value 8 * 4 marks a pair slot without a live pair; the number of live pairs differs from owner to owner, and some owner has all 16 slots live.
All inputs are finite; a program needn't handle non-finite values.
Results may differ from a plain program's by a relative error of at most 0.011.
Values may be sent and summed in bfloat16 or wider, within the bound.
A program may use at most 64 MiB of HBM per device.

v0:
```python
import math

import jax
import jax.numpy as jnp
from jax import lax
from jax.sharding import PartitionSpec as P


def make_tables(side_len):
    ticks = jnp.arange(side_len, dtype=jnp.int32)
    product = ticks[:, None] * ticks[None, :] % side_len
    angle = 2.0 * math.pi / side_len * product.astype(jnp.float32)
    cosine = jnp.cos(angle) / math.sqrt(side_len)
    sine = jnp.sin(angle) / math.sqrt(side_len)
    coord = ticks.astype(jnp.float32)
    gap = coord[:, None] - coord[None, :]
    narrow = jnp.exp(-gap * gap / (2.0 * 0.35 * 0.35)) / (0.35 * math.sqrt(2.0 * math.pi))
    broad = jnp.exp(-gap * gap / 32.0) / (4.0 * math.sqrt(2.0 * math.pi))
    band = narrow - broad
    lag = jnp.where(coord < side_len / 2, coord, coord - side_len)
    return (cosine.astype(jnp.bfloat16), sine.astype(jnp.bfloat16), band.astype(jnp.bfloat16), lag)


def band_pass(stack, band):
    partial_value = jnp.einsum(
        "ij,bjk->bik", band, stack, preferred_element_type=jnp.float32
    ).astype(jnp.bfloat16)
    return jnp.einsum(
        "bij,kj->bik", partial_value, band, preferred_element_type=jnp.float32
    ).astype(jnp.bfloat16)


def prepare(stack, tables):
    cosine, sine, band, lag = tables
    filtered = band_pass(stack, band)
    left = jnp.concatenate([cosine, sine], 0)
    return jnp.einsum("ij,bjk->bik", left, filtered, preferred_element_type=jnp.float32).astype(
        jnp.bfloat16
    )


def finish(halves, tables):
    cosine, sine, band, lag = tables
    side_len = halves.shape[-1]
    count = halves.shape[0] // 2
    right = jnp.concatenate([cosine, sine], 1)
    back_left = jnp.concatenate([cosine, -sine], 1)
    quarter = jnp.einsum("bij,jk->bik", halves, right, preferred_element_type=jnp.float32)
    real_part = quarter[:, :side_len, :side_len] - quarter[:, side_len:, side_len:]
    imag_part = -(quarter[:, :side_len, side_len:] + quarter[:, side_len:, :side_len])
    moving_real, fixed_real = (real_part[:count], real_part[count:])
    moving_imag, fixed_imag = (imag_part[:count], imag_part[count:])
    power_real = moving_real * fixed_real + moving_imag * fixed_imag
    power_imag = moving_imag * fixed_real - moving_real * fixed_imag
    power = jnp.concatenate([power_real, power_imag], 1).astype(jnp.bfloat16)
    mixed = jnp.einsum("bij,jk->bik", power, right, preferred_element_type=jnp.float32)
    first = mixed[:, :side_len, :side_len] - mixed[:, side_len:, side_len:]
    second = mixed[:, :side_len, side_len:] + mixed[:, side_len:, :side_len]
    stacked = jnp.concatenate([first, second], 1).astype(jnp.bfloat16)
    surface = jnp.einsum("ij,bjk->bik", back_left, stacked, preferred_element_type=jnp.float32)
    weight = surface * surface
    denom = jnp.mean(weight, axis=(1, 2)) + 1e-06
    flow_y = jnp.mean(lag[None, :, None] * weight, axis=(1, 2)) / denom
    flow_x = jnp.mean(lag[None, None, :] * weight, axis=(1, 2)) / denom
    return jnp.stack([flow_y, flow_x], 0)


def per_device(patches, send_index, pair_slots, node_links):
    side_len = patches.shape[-1]
    patch_count = patches.shape[0]
    pair_count = pair_slots.shape[-1]
    tile_count = lax.axis_size("tiles")
    tables = make_tables(side_len)
    wanted = send_index[0]
    capacity = wanted.shape[0] // tile_count
    present = wanted < patch_count
    safe_wanted = jnp.minimum(wanted, patch_count - 1)
    picked = patches[safe_wanted]
    picked = jnp.where(present[:, None, None], picked, jnp.zeros_like(picked))
    received = lax.all_to_all(
        picked.reshape((tile_count, capacity) + patches.shape[1:]),
        "tiles",
        split_axis=0,
        concat_axis=0,
        tiled=True,
    )
    slot_total = tile_count * capacity
    received = received.reshape((slot_total,) + received.shape[2:])
    slots = pair_slots[0].reshape(-1)
    valid = slots < slot_total
    chosen = received[jnp.minimum(slots, slot_total - 1)]
    chosen = jnp.where(valid[:, None, None], chosen, jnp.zeros_like(chosen))
    block = min(16, pair_count)
    moving = chosen[:pair_count].reshape((pair_count // block, block) + chosen.shape[1:])
    fixed = chosen[pair_count:].reshape((pair_count // block, block) + chosen.shape[1:])

    def per_block(item):
        moving_part, fixed_part = item
        both = jnp.concatenate([moving_part, fixed_part], 0)
        both = prepare(both, tables)
        return finish(both, tables)

    flows = lax.map(per_block, (moving, fixed))
    pair_flow = jnp.transpose(flows, (1, 0, 2)).reshape(2, pair_count)
    flow_rows = lax.all_gather(pair_flow, "mesh", axis=1, tiled=True)
    linked = flow_rows[:, node_links[0]]
    relaxed = 0.5 * linked[:, 0] + 0.5 * jnp.mean(linked[:, 1:], axis=1)
    return (pair_flow, relaxed)


def solution(mesh):
    placed = (
        P(("parts", "tiles", "mesh"), None, None),
        P(("parts", "tiles", "mesh"), None),
        P(("parts", "tiles", "mesh"), None, None),
        P(("parts", "tiles", "mesh"), None, None),
    )
    return jax.shard_map(
        per_device,
        mesh=mesh,
        in_specs=placed,
        out_specs=(P(None, ("parts", "tiles", "mesh")), P(None, ("parts", "tiles", "mesh"))),
        check_vma=False,
    )
```

profile of v0, /device:TPU:0, one launch (start us, length us, event | category | flops | bytes accessed | tf_op | source)
XLA Modules:
  0.0 55.5 jit_solution(8383764545167968574)
XLA Ops:
  0.6 0.0 copy-start
  0.6 0.7 %fusion.57 = s32[32]{0:T(128)S(1)} fusion(s32[1,32]{1,0:T(1,128)} %param.5), kind=kLoop, calls=%fused_computation.76 | loop fusion | flops 128 | bytes 256 | tf_op jit(solution)/shard_map/select_n | solution.py:78
  1.4 0.7 %compare_reduce_fusion = pred[32]{0:T(512)(128)(4,1)S(1)} fusion(s32[1,32]{1,0:T(1,128)} %param.5), kind=kLoop, calls=%fused_computation.71 | loop fusion | flops 32 | bytes 160 | tf_op jit(solution)/shard_map/lt | solution.py:76
  2.1 0.1 lt.91
  2.2 0.0 copy-done
  2.2 0.8 %gather_fusion = bf16[32,128,128]{2,1,0:T(8,128)(2,1)S(1)} fusion(bf16[32,128,128]{2,1,0:T(8,128)(2,1)S(1)} %copy-done, s32[1024]{0:T(1024)S(1)} %pad_clamp_fusion.2), kind=kCustom, calls=%fused_computation | custom fusion | bytes 2097280 | tf_op jit(solution)/shard_map/gather | solution.py:78
  2.9 0.0 copy-start.2
  2.9 0.0 copy-start.1
  2.9 1.1 %broadcast_select_fusion = bf16[8,4,128,128]{3,2,1,0:T(8,128)(2,1)} fusion(bf16[8,4,128,128]{3,2,1,0:T(8,128)(2,1)S(1)} %bitcast.55, pred[8,4]{1,0:T(8,128)(4,1)S(1)} %lt.91), kind=kLoop, calls=%fused_computation.31 | loop fusion | flops 524288 | bytes 2097184 | tf_op jit(solution)/shard_map/jit(_where)/select_n | solution.py:79
  4.1 7.3 %all-to-all-start = ((bf16[8,4,128,128]{3,2,1,0:T(8,128)(2,1)}), bf16[8,4,128,128]{3,2,1,0:T(8,128)(2,1)S(1)}, u32[]{:S(2)}, u32[]{:S(2)}) async-start(bf16[8,4,128,128]{3,2,1,0:T(8,128)(2,1)} %broadcast_select_fusion), calls=%async_computation | async-start | bytes 2097152 | tf_op jit(solution)/shard_map/all_to_all | solution.py:80
  11.3 0.0 copy-done.2
  11.4 0.1 min.29
  11.4 0.1 lt.89
  11.6 0.0 copy-done.1
  11.6 0.3 fusion.53
  11.9 0.3 multiply_convert_fusion
  12.1 25.0 %all-to-all-done = bf16[8,4,128,128]{3,2,1,0:T(8,128)(2,1)S(1)} async-done(((bf16[8,4,128,128]{3,2,1,0:T(8,128)(2,1)}), bf16[8,4,128,128]{3,2,1,0:T(8,128)(2,1)S(1)}, u32[]{:S(2)}, u32[]{:S(2)}) %all-to-all-start) | async-done | bytes 1048608 | tf_op jit(solution)/shard_map/all_to_all | solution.py:80
  37.1 0.7 %gather_fusion.1 = bf16[32,128,128]{2,1,0:T(8,128)(2,1)S(1)} fusion(bf16[32,128,128]{2,1,0:T(8,128)(2,1)S(1)} %bitcast.54, s32[1024]{0:T(1024)S(1)} %pad_clamp_fusion.1), kind=kCustom, calls=%fused_computation.1 | custom fusion | bytes 2097280 | tf_op jit(solution)/shard_map/gather | solution.py:91
  37.9 1.3 %convolution_convert_fusion = bf16[32,128,128]{2,1,0:T(8,128)(2,1)S(1)} fusion(bf16[32,128,128]{2,1,0:T(8,128)(2,1)S(1)} %gather_fusion.1, pred[32]{0:T(512)(128)(4,1)S(1)} %lt.89, f32[128]{0:T(128)S(1)} %iota_convert_fusion), kind=kOutput, calls=%fused_computation.11 | convolution fusion | flops 270303232 | bytes 2097696 | tf_op jit(solution)/shard_map/while/body/eval_jaxpr/bij,kj->bik/dot_general | solution.py:28
  39.2 5.8 %fusion.1 = f32[32,256,256]{2,1,0:T(8,128)} fusion(bf16[32,128,128]{2,1,0:T(8,128)(2,1)S(1)} %convolution_convert_fusion, bf16[128,128]{1,0:T(8,128)(2,1)S(1)} %get-tuple-element.37, bf16[128,128]{1,0:T(8,128)(2,1)S(1)} %get-tuple-element.38), kind=kOutput, calls=%fused_computation.6 | convolution fusion | flops 806617088 | bytes 9502720 | tf_op jit(solution)/shard_map/while/body/eval_jaxpr/bij,jk->bik/dot_general | solution.py:48
  44.9 4.4 %slice_subtract_fusion = (f32[32,128,128]{2,1,0:T(8,128)S(1)}, f32[32,128,128]{2,1,0:T(8,128)S(1)}) fusion(f32[32,256,256]{2,1,0:T(8,128)} %fusion.1), kind=kLoop, calls=%fused_computation.5 | loop fusion | flops 1572864 | bytes 12582912 | tf_op jit(solution)/shard_map/while/body/eval_jaxpr/sub | solution.py:49
  49.3 0.4 add_convert_fusion
  49.7 0.7 %fusion.9 = f32[16,256,256]{2,1,0:T(8,128)S(1)} fusion(bf16[16,128,128]{2,1,0:T(8,128)(2,1)S(1)} %get-tuple-element.34, bf16[16,128,128]{2,1,0:T(8,128)(2,1)S(1)} %get-tuple-element.33, bf16[128,128]{1,0:T(8,128)(2,1)S(1)} %get-tuple-element.38, bf16[128,128]{1,0:T(8,128)(2,1)S(1)} %get-tuple-element.37), kind=kOutput, calls=%fused_computation.18 | convolution fusion | flops 270663680 | bytes 5308416 | tf_op jit(solution)/shard_map/while/body/eval_jaxpr/bij,jk->bik/dot_general | solution.py:56
  50.4 0.3 fusion.8
  50.7 0.6 %multiply_reduce_fusion.1 = (f32[16]{0:T(128)S(1)}, f32[16]{0:T(128)S(1)}, f32[16]{0:T(128)S(1)}) fusion(f32[128]{0:T(128)S(1)} %compare_select_fusion.3, bf16[128,128]{1,0:T(8,128)(2,1)S(1)} %get-tuple-element.38, bf16[128,128]{1,0:T(8,128)(2,1)S(1)} %fusion.53, bf16[16,128,128]{2,1,0:T(8,128)(2,1)S(1)} %get-tuple-element.32, ...), kind=kOutput, calls=%fused_computation.26 | convolution fusion | flops 138018768 | bytes 1114816 | tf_op jit(solution)/shard_map/while/body/eval_jaxpr/ij,bjk->bik/dot_general | solution.py:60
  51.4 0.6 %pad_maximum_fusion.2 = f32[2,16]{1,0:T(2,128)} fusion(f32[1,16]{1,0:T(1,128)S(1)} %get-tuple-element.36, f32[1,16]{1,0:T(1,128)S(1)} %get-tuple-element.35), kind=kLoop, calls=%fused_computation.75 | loop fusion | flops 32 | bytes 256 | tf_op jit(solution)/shard_map/while/body/eval_jaxpr/stack | solution.py:65
  51.9 1.8 %all-gather = f32[2,16,2]{1,2,0:T(2,128)S(1)} all-gather(f32[1,16,2]{1,2,0:T(2,128)S(1)} %fusion.76), channel_id=1, replica_groups=mesh['parts'=2,'tiles'=8,'mesh'=2] {'mesh'}, dimensions={0}, use_global_device_ids=true | all-gather | bytes 384 | tf_op jit(solution)/shard_map/all_gather | solution.py:105
  53.7 0.1 copy.34
  53.8 1.0 %gather_fusion.2 = f32[512,2]{1,0:T(8,128)S(1)} fusion(f32[2,32]{0,1:T(8,128)S(1)} %bitcast.57, s32[1024]{0:T(1024)S(1)} %pad_clamp_fusion), kind=kCustom, calls=%fused_computation.2 | custom fusion | bytes 10240 | tf_op jit(solution)/shard_map/gather | solution.py:106
  54.8 0.1 copy.28
  54.9 0.6 %fusion.56 = f32[2,128]{1,0:T(2,128)} fusion(f32[2,4,128]{2,0,1:T(2,128)S(1)} %bitcast.59, f32[2,128]{1,0:T(2,128)S(1)} %slice_reduce_fusion), kind=kLoop, calls=%fused_computation.74 | loop fusion | flops 768 | bytes 3072 | tf_op jit(solution)/shard_map/add | solution.py:107
  (12 shorter events, 0.1 us)
Async XLA Ops:
  0.6 1.5 %copy-start = (bf16[32,128,128]{2,1,0:T(8,128)(2,1)S(1)}, bf16[32,128,128]{2,1,0:T(8,128)(2,1)}, u32[]{:S(2)}) copy-start(bf16[32,128,128]{2,1,0:T(8,128)(2,1)} %param.4) | copy-start | bytes 3145732
  2.9 8.4 %copy-start.2 = (s32[1,2,16]{2,1,0:T(2,128)S(1)}, s32[1,2,16]{2,1,0:T(2,128)}, u32[]{:S(2)}) copy-start(s32[1,2,16]{2,1,0:T(2,128)} %param.6) | copy-start | bytes 388
  2.9 8.6 %copy-start.1 = (s32[1,4,128]{2,1,0:T(4,128)S(1)}, s32[1,4,128]{2,1,0:T(4,128)}, u32[]{:S(2)}) copy-start(s32[1,4,128]{2,1,0:T(4,128)} %param.7) | copy-start | bytes 6148
  4.1 33.0 %all-to-all-start = ((bf16[8,4,128,128]{3,2,1,0:T(8,128)(2,1)}), bf16[8,4,128,128]{3,2,1,0:T(8,128)(2,1)S(1)}, u32[]{:S(2)}, u32[]{:S(2)}) async-start(bf16[8,4,128,128]{3,2,1,0:T(8,128)(2,1)} %broadcast_select_fusion), calls=%async_computation | async-start | bytes 2097152 | tf_op jit(solution)/shard_map/all_to_all | solution.py:80
where the time goes:
time: 55.7 us; the launch traced here: 55.5 us
  waiting for transfers between devices  25 us (45%)
  other arithmetic  9.36 us (17%)
  matrix products  8.41 us (15%)
  starting transfers between devices  7.25 us (13%)
  local copies, waits for them, and re-layouts  3 us (5%)
  blocking collectives  1.77 us (3%)
  between operations  0.78 us (1%)
    all_to_all x1, waiting for transfers between devices, per_device(): lax.all_to_all(picked.reshape((tile_count, capacity) + patches.shape[1:])...  25 us
    all_to_all x1, starting transfers between devices, per_device(): lax.all_to_all(picked.reshape((tile_count, capacity) + patches.shape[1:])...  7.25 us
    dot_general x1, matrix products, finish(): jnp.einsum('bij,jk->bik', halves, right, preferred_element_type=jnp.float32)  5.76 us
    sub x1, other arithmetic, finish(): quarter[:, :side_len, :side_len] - quarter[:, side_len:, side_len:]  4.35 us
    all_gather x1, blocking collectives, per_device(): flow_rows = lax.all_gather(pair_flow, 'mesh', axis=1, tiled=True)  1.77 us
    dot_general x1, matrix products, band_pass(): jnp.einsum('bij,kj->bik', partial_value, band, preferred_element_type=jnp...  1.31 us
    gather x2, local copies, waits for them, and re-layouts, per_device(): linked = flow_rows[:, node_links[0]]  1.14 us
    select_n x1, other arithmetic, per_device(): picked = jnp.where(present[:, None, None], picked, jnp.zeros_like(picked))  1.13 us
  transfers between devices with their start and end apart: 1, of which 1 were waited for; matrix products, arithmetic and copies ran while one was open for 1% of the time, Pallas kernels for 0%

commit v1 on v0

v1 whole, which is shorter than its diff:
```python
import functools
import math

import jax
import jax.numpy as jnp
import ml_dtypes
import numpy as np
from jax import lax
from jax.experimental import pallas as pl
from jax.experimental.pallas import tpu as pltpu
from jax.sharding import PartitionSpec as P

MESH = pl.DeviceIdType.MESH
BF16 = jnp.bfloat16
F32 = jnp.float32


def make_tables(side_len):
    ticks = np.arange(side_len)
    product = ticks[:, None] * ticks[None, :] % side_len
    angle = np.float32(2.0 * math.pi / side_len) * product.astype(np.float32)
    root = math.sqrt(side_len)
    cosine = (np.cos(angle) / root).astype(np.float32).astype(ml_dtypes.bfloat16)
    sine = (np.sin(angle) / root).astype(np.float32).astype(ml_dtypes.bfloat16)
    coord = ticks.astype(np.float32)
    gap = coord[:, None] - coord[None, :]
    narrow = np.exp(-gap * gap / (2.0 * 0.35 * 0.35)) / (0.35 * math.sqrt(2.0 * math.pi))
    broad = np.exp(-gap * gap / 32.0) / (4.0 * math.sqrt(2.0 * math.pi))
    band = (narrow - broad).astype(np.float32).astype(ml_dtypes.bfloat16)
    lag = np.where(coord < side_len / 2, coord, coord - side_len).astype(np.float32)
    return cosine, sine, band, lag


def other_of(me, step, count):
    if count & (count - 1):
        raise ValueError("tiles: not 2**n")
    partner = 0
    bit = 1
    while bit < count:
        partner = partner + (me // bit + step // bit) % 2 * bit
        bit *= 2
    return partner


def dot(left, right):
    return jnp.dot(left, right, preferred_element_type=F32)


def kernel(
    tile_count,
    mesh_count,
    send_index,
    pair_slots,
    links,
    patches_hbm,
    band_hbm,
    left_hbm,
    right_hbm,
    back_hbm,
    final_hbm,
    lag_hbm,
    pair_out,
    relaxed_out,
    patches,
    band,
    left,
    right,
    back,
    final,
    lag,
    stage,
    recv,
    spectrum,
    sums,
    flows,
    load_sem,
    send_sem,
    recv_sem,
    flow_send_sem,
    flow_recv_sem,
):
    me = lax.axis_index("tiles")
    lane = lax.axis_index("mesh")
    patch_count = patches.shape[0]
    side = patches.shape[-1]
    slot_total = recv.shape[0]
    capacity = slot_total // tile_count
    pair_count = pair_slots.shape[-1]

    fetch = [
        pltpu.make_async_copy(src, dst, load_sem.at[n])
        for n, (src, dst) in enumerate(
            (
                (patches_hbm, patches),
                (band_hbm, band),
                (left_hbm, left),
                (right_hbm, right),
                (back_hbm, back),
                (final_hbm, final),
                (lag_hbm, lag),
            )
        )
    ]
    for copy in fetch:
        copy.start()

    barrier = pltpu.get_barrier_semaphore()

    def greet(step, carry):
        pl.semaphore_signal(
            barrier, inc=1, device_id={"tiles": other_of(me, step, tile_count)}, device_id_type=MESH
        )
        return carry

    lax.fori_loop(1, tile_count, greet, 0)
    for hop in range(1, mesh_count):
        pl.semaphore_signal(
            barrier, inc=1, device_id={"mesh": lax.rem(lane + hop, mesh_count)}, device_id_type=MESH
        )
    fetch[0].wait()

    def picked(step, slot):
        index = send_index[0, other_of(me, step, tile_count) * capacity + slot]
        block = patches[jnp.minimum(index, patch_count - 1)]
        return jnp.where(index < patch_count, block, jnp.zeros_like(block))

    def sending(step):
        block = pl.ds(step * capacity, capacity)
        return pltpu.make_async_remote_copy(
            src_ref=stage.at[block],
            dst_ref=recv.at[block],
            send_sem=send_sem.at[step],
            recv_sem=recv_sem.at[step],
            device_id={"tiles": other_of(me, step, tile_count)},
            device_id_type=MESH,
        )

    def fill(step):
        for slot in range(capacity):
            stage[step * capacity + slot] = picked(step, slot)

    fill(tile_count - 1)
    pl.semaphore_wait(barrier, tile_count + mesh_count - 2)
    sending(tile_count - 1).start()

    def send(turn, carry):
        step = tile_count - 1 - turn
        fill(step)
        sending(step).start()
        return carry

    lax.fori_loop(1, tile_count - 1, send, 0)
    for slot in range(capacity):
        recv[slot] = picked(0, slot)

    for copy in fetch[1:]:
        copy.wait()

    def prepare(step):
        blocks = [recv[step * capacity + slot] for slot in range(capacity)]
        width = 2 if capacity % 2 == 0 else 1
        for first in range(0, capacity, width):
            wide = jnp.concatenate(blocks[first : first + width], 1)
            partial = dot(band[...], wide).astype(BF16)
            tall = jnp.concatenate([partial[:, n * side : (n + 1) * side] for n in range(width)], 0)
            filtered = dot(tall, band[...]).astype(BF16)
            wide = jnp.concatenate([filtered[n * side : (n + 1) * side] for n in range(width)], 1)
            halves = dot(left[...], wide).astype(BF16)
            for n in range(width):
                columns = halves[:, n * side : (n + 1) * side]
                both = jnp.concatenate([columns[:side], columns[side:]], 1)
                spectrum[step * capacity + first + n] = dot(both, right[...])

    prepare(0)
    half = tile_count // 2

    def take(turn, carry):
        step = jnp.where(turn < half, turn, tile_count - 1 - (turn - half))
        sending(step).wait_recv()
        prepare(step)
        return carry

    lax.fori_loop(1, tile_count, take, 0)

    def place(slot):
        return other_of(me, slot // capacity, tile_count) * capacity + slot % capacity

    group = 2 if pair_count % 2 == 0 else 1

    def finish(turn, carry):
        backs = []
        lives = []
        for n in range(group):
            pair = turn * group + n
            moving_slot = pair_slots[0, 0, pair]
            fixed_slot = pair_slots[0, 1, pair]
            live = jnp.logical_and(moving_slot < slot_total, fixed_slot < slot_total)
            lives.append(jnp.where(live, 1.0, 0.0).astype(F32))
            moving = spectrum[place(jnp.minimum(moving_slot, slot_total - 1))]
            fixed = spectrum[place(jnp.minimum(fixed_slot, slot_total - 1))]
            mr, mi = moving[:, :side], moving[:, side:]
            fr, fi = fixed[:, :side], fixed[:, side:]
            power = jnp.concatenate([mr * fr + mi * fi, mi * fr - mr * fi], 1).astype(BF16)
            mixed = dot(power, back[...]).astype(BF16)
            backs.append(jnp.concatenate([mixed[:, :side], mixed[:, side:]], 0))
        surface = dot(final[...], jnp.concatenate(backs, 1))
        weight = surface * surface
        for n in range(group):
            part = weight[:, n * side : (n + 1) * side]
            pair = turn * group + n
            sums[0, pl.ds(pair, 1), :] = lives[n] * jnp.sum(part, axis=0, keepdims=True)
            sums[1, pl.ds(pair, 1), :] = lives[n] * jnp.sum(lag[:side] * part, axis=0, keepdims=True)
        return carry

    lax.fori_loop(0, pair_count // group, finish, 0)

    scale = 1.0 / (side * side)
    total = sums[0]
    denom = jnp.sum(total, axis=1, keepdims=True) * scale + 1e-06
    flow_y = jnp.sum(sums[1], axis=1, keepdims=True) * scale / denom
    flow_x = jnp.sum(total * lag[side : side + 1], axis=1, keepdims=True) * scale / denom
    own = [jnp.broadcast_to(flow_y, (pair_count, side)), jnp.broadcast_to(flow_x, (pair_count, side))]
    flows[lane, 0] = own[0]
    flows[lane, 1] = own[1]
    exchange = [
        pltpu.make_async_remote_copy(
            src_ref=flows.at[lane],
            dst_ref=flows.at[lane],
            send_sem=flow_send_sem.at[hop],
            recv_sem=flow_recv_sem.at[hop],
            device_id={"mesh": lax.rem(lane + hop, mesh_count)},
            device_id_type=MESH,
        )
        for hop in range(1, mesh_count)
    ]
    for copy in exchange:
        copy.start()
    rows = lax.broadcasted_iota(jnp.int32, (pair_count, side), 0)
    columns = lax.broadcasted_iota(jnp.int32, (pair_count, side), 1)
    for axis in range(2):
        line = jnp.sum(jnp.where(rows == columns, own[axis], 0.0), axis=0, keepdims=True)
        pair_out[pl.ds(axis, 1), :] = line[:, :pair_count]

    nodes = links.shape[-1]
    link_count = links.shape[1]
    rows = lax.broadcasted_iota(jnp.int32, (mesh_count * pair_count, nodes), 0)
    shares = jnp.where(rows == links[0, 0:1, :], 0.5, 0.0)
    for number in range(1, link_count):
        hit = rows == links[0, number : number + 1, :]
        shares = shares + jnp.where(hit, 0.5 / (link_count - 1), 0.0)
    for copy in exchange:
        copy.wait()
    for axis in range(2):
        line = jnp.zeros((1, nodes), F32)
        for number in range(mesh_count):
            part = shares[number * pair_count : (number + 1) * pair_count]
            line = line + jnp.sum(part * flows[number, axis][:, :nodes], axis=0, keepdims=True)
        relaxed_out[pl.ds(axis, 1), :] = line

    def drain(step, carry):
        sending(step).wait_send()
        return carry

    lax.fori_loop(1, tile_count, drain, 0)


def per_device(patches, send_index, pair_slots, node_links):
    patch_count, side, _ = patches.shape
    slot_total = send_index.shape[1]
    pair_count = pair_slots.shape[-1]
    nodes = node_links.shape[-1]
    tile_count = lax.axis_size("tiles")
    mesh_count = lax.axis_size("mesh")
    cosine, sine, band, lag = make_tables(side)
    left = np.concatenate([cosine, sine], 0)
    right = np.block([[cosine, -sine], [-sine, -cosine]])
    back = np.block([[cosine, sine], [-sine, cosine]])
    final = np.concatenate([cosine, -sine], 1)
    lags = np.zeros((side + 8, side), np.float32)
    lags[:side] = lag[:, None]
    lags[side:] = lag[None, :]
    tables = [jnp.asarray(table) for table in (band, left, right, back, final, lags)]
    smem = pl.BlockSpec(memory_space=pltpu.SMEM)
    vmem = pl.BlockSpec(memory_space=pltpu.VMEM)
    hbm = pl.BlockSpec(memory_space=pl.ANY)
    scratch = [
        pltpu.VMEM(patches.shape, BF16),
        *[pltpu.VMEM(table.shape, table.dtype) for table in tables],
        pltpu.VMEM((slot_total, side, side), BF16),
        pltpu.VMEM((slot_total, side, side), BF16),
        pltpu.VMEM((slot_total, side, 2 * side), F32),
        pltpu.VMEM((2, pair_count, side), F32),
        pltpu.VMEM((mesh_count, 2, pair_count, side), F32),
        pltpu.SemaphoreType.DMA((1 + len(tables),)),
        pltpu.SemaphoreType.DMA((tile_count,)),
        pltpu.SemaphoreType.DMA((tile_count,)),
        pltpu.SemaphoreType.DMA((mesh_count,)),
        pltpu.SemaphoreType.DMA((mesh_count,)),
    ]
    return pl.pallas_call(
        functools.partial(kernel, tile_count, mesh_count),
        out_shape=(
            jax.ShapeDtypeStruct((2, pair_count), F32),
            jax.ShapeDtypeStruct((2, nodes), F32),
        ),
        in_specs=[smem, smem, vmem, hbm] + [hbm] * len(tables),
        out_specs=(vmem, vmem),
        scratch_shapes=scratch,
        compiler_params=pltpu.CompilerParams(
            collective_id=0, has_side_effects=True, vmem_limit_bytes=48 * 2**20
        ),
        name="flow",
    )(send_index, pair_slots, node_links, patches, *tables)


def solution(mesh):
    spread = ("parts", "tiles", "mesh")
    placed = (
        P(spread, None, None),
        P(spread, None),
        P(spread, None, None),
        P(spread, None, None),
    )
    return jax.shard_map(
        per_device,
        mesh=mesh,
        in_specs=placed,
        out_specs=(P(None, spread), P(None, spread)),
        check_vma=False,
    )
```

time: 55.7 us -> 47.1 us (0.85)
  Pallas kernels: 0 us -> 36.5 us
  waiting for transfers between devices: 25 us -> 0 us
  other arithmetic: 9.36 us -> 0 us
  matrix products: 8.41 us -> 0 us
  starting transfers between devices: 7.25 us -> 0 us
  local copies, waits for them, and re-layouts: 3 us -> 9.48 us
  blocking collectives: 1.77 us -> 0 us
    pallas_call x0 -> x1, Pallas kernels: none -> 36.5 us  [per_device(): pl.pallas_call(functools.partial(kernel, tile_count, mesh_count), out_sha...]
    all_to_all x1 -> x0, waiting for transfers between devices: 25 us -> none  [per_device(): lax.all_to_all(picked.reshape((tile_count, capacity) + patches.shape[1:])...]
    unnamed x7 -> x22, local copies, waits for them, and re-layouts: 0.11 us -> 9.48 us
    dot_general x4 -> x0, matrix products: 8.41 us -> none  [the longest x1 5.76 us: finish(): jnp.einsum('bij,jk->bik', halves, right, preferred_element_type=jnp.float32)]
    all_to_all x1 -> x0, starting transfers between devices: 7.25 us -> none  [per_device(): lax.all_to_all(picked.reshape((tile_count, capacity) + patches.shape[1:])...]
    sub x1 -> x0, other arithmetic: 4.35 us -> none  [finish(): quarter[:, :side_len, :side_len] - quarter[:, side_len:, side_len:]]
    gather x4 -> x0, local copies, waits for them, and re-layouts: 2.64 us -> none  [the longest x2 1.14 us: per_device(): linked = flow_rows[:, node_links[0]]]
    select_n x5 -> x0, other arithmetic: 1.89 us -> none  [the longest x1 1.13 us: per_device(): picked = jnp.where(present[:, None, None], picked, jnp.zeros_like(picked))]
  transfers between devices with their start and end apart: 1 -> 0, of which waited for: 1 -> 0; matrix products, arithmetic and copies ran while one was open for 1% -> 0% of each run, Pallas kernels for 0% -> 0%
where the time goes in v1:
time: 47.1 us; the launch traced here: 46.6 us
  Pallas kernels  36.5 us (77%)
  local copies, waits for them, and re-layouts  9.48 us (20%)
  between operations  0.66 us (1%)
    pallas_call x1, Pallas kernels, per_device(): pl.pallas_call(functools.partial(kernel, tile_count, mesh_count), out_sha...  36.5 us
    unnamed x22, local copies, waits for them, and re-layouts  9.48 us

profile of v1, /device:TPU:0, one launch (start us, length us, event | category | flops | bytes accessed | tf_op | source)
XLA Modules:
  0.0 46.6 jit_solution(9922526487134335472)
XLA Ops:
  0.6 0.0 copy-start
  0.6 1.2 %copy-done = bf16[32,128,128]{2,1,0:T(8,128)(2,1)S(1)} copy-done((bf16[32,128,128]{2,1,0:T(8,128)(2,1)S(1)}, bf16[32,128,128]{2,1,0:T(8,128)(2,1)}, u32[]{:S(2)}) %copy-start) | copy-done | bytes 1048600
  1.9 0.0 copy-start.1
  1.9 0.9 %copy-done.1 = bf16[256,256]{1,0:T(8,128)(2,1)S(1)} copy-done((bf16[256,256]{1,0:T(8,128)(2,1)S(1)}, bf16[256,256]{1,0:T(8,128)(2,1)}, u32[]{:S(2)}) %copy-start.1) | copy-done | bytes 131096
  2.8 0.0 copy-start.2
  2.8 0.9 %copy-done.2 = bf16[256,256]{1,0:T(8,128)(2,1)S(1)} copy-done((bf16[256,256]{1,0:T(8,128)(2,1)S(1)}, bf16[256,256]{1,0:T(8,128)(2,1)}, u32[]{:S(2)}) %copy-start.2) | copy-done | bytes 131096
  3.7 0.0 copy-start.3
  3.7 0.9 %copy-done.3 = f32[136,128]{1,0:T(8,128)S(1)} copy-done((f32[136,128]{1,0:T(8,128)S(1)}, f32[136,128]{1,0:T(8,128)}, u32[]{:S(2)}) %copy-start.3) | copy-done | bytes 69656
  4.5 0.0 copy-start.4
  4.6 0.8 %copy-done.4 = bf16[128,256]{1,0:T(8,128)(2,1)S(1)} copy-done((bf16[128,256]{1,0:T(8,128)(2,1)S(1)}, bf16[128,256]{1,0:T(8,128)(2,1)}, u32[]{:S(2)}) %copy-start.4) | copy-done | bytes 65560
  5.4 0.0 copy-start.5
  5.4 0.8 %copy-done.5 = bf16[256,128]{1,0:T(8,128)(2,1)S(1)} copy-done((bf16[256,128]{1,0:T(8,128)(2,1)S(1)}, bf16[256,128]{1,0:T(8,128)(2,1)}, u32[]{:S(2)}) %copy-start.5) | copy-done | bytes 65560
  6.2 0.0 copy-start.6
  6.2 0.8 %copy-done.6 = bf16[128,128]{1,0:T(8,128)(2,1)S(1)} copy-done((bf16[128,128]{1,0:T(8,128)(2,1)S(1)}, bf16[128,128]{1,0:T(8,128)(2,1)}, u32[]{:S(2)}) %copy-start.6) | copy-done | bytes 32792
  7.0 0.0 copy-start.7
  7.0 0.7 %copy-done.7 = s32[1,4,128]{2,1,0:T(4,128)S(1)} copy-done((s32[1,4,128]{2,1,0:T(4,128)S(1)}, s32[1,4,128]{2,1,0:T(4,128)}, u32[]{:S(2)}) %copy-start.7) | copy-done | bytes 2072
  7.7 0.0 copy-start.8
  7.7 0.7 %copy-done.8 = s32[1,2,16]{2,1,0:T(2,128)S(1)} copy-done((s32[1,2,16]{2,1,0:T(2,128)S(1)}, s32[1,2,16]{2,1,0:T(2,128)}, u32[]{:S(2)}) %copy-start.8) | copy-done | bytes 152
  8.3 0.0 copy-start.9
  8.4 0.7 %copy-done.9 = s32[1,32]{1,0:T(1,128)S(1)} copy-done((s32[1,32]{1,0:T(1,128)S(1)}, s32[1,32]{1,0:T(1,128)}, u32[]{:S(2)}) %copy-start.9) | copy-done | bytes 152
  9.0 36.5 %flow.1 = (f32[2,16]{1,0:T(2,128)S(1)}, f32[2,128]{1,0:T(2,128)S(1)}) custom-call(s32[1,32]{1,0:T(1,128)S(1)} %copy-done.9, s32[1,2,16]{2,1,0:T(2,128)S(1)} %copy-done.8, s32[1,4,128]{2,1,0:T(4,128)S(1)} %copy-done.7, bf16[32,128,128]{2,1,0:T(8,128)(2,1)S(1)} %copy-done, bf16[128,128]{1,0:T(8,128)(2,1)S(1)} %copy-done.6, bf16[256,128]{1,0:T(8,128)(2,1)S(1)} %copy-done.5, ...), custom_call_target="tpu_custom_call" | custom-call | tf_op jit(solution)/shard_map/flow/pallas_call | solution.py:300
  45.5 0.6 %copy.14 = f32[2,16]{1,0:T(2,128)} copy(f32[2,16]{1,0:T(2,128)S(1)} %get-tuple-element.4) | data formatting | bytes 256
  46.0 0.6 %copy.15 = f32[2,128]{1,0:T(2,128)} copy(f32[2,128]{1,0:T(2,128)S(1)} %get-tuple-element.5) | data formatting | bytes 2048
Async XLA Ops:
  0.6 1.2 %copy-start = (bf16[32,128,128]{2,1,0:T(8,128)(2,1)S(1)}, bf16[32,128,128]{2,1,0:T(8,128)(2,1)}, u32[]{:S(2)}) copy-start(bf16[32,128,128]{2,1,0:T(8,128)(2,1)} %patches_hbm.1) | copy-start | bytes 3145732
  1.9 0.9 %copy-start.1 = (bf16[256,256]{1,0:T(8,128)(2,1)S(1)}, bf16[256,256]{1,0:T(8,128)(2,1)}, u32[]{:S(2)}) copy-start(bf16[256,256]{1,0:T(8,128)(2,1)} %constant.15.clone.back_hbm) | copy-start | bytes 393220
  2.8 0.9 %copy-start.2 = (bf16[256,256]{1,0:T(8,128)(2,1)S(1)}, bf16[256,256]{1,0:T(8,128)(2,1)}, u32[]{:S(2)}) copy-start(bf16[256,256]{1,0:T(8,128)(2,1)} %constant.14.clone.right_hbm) | copy-start | bytes 393220
  3.7 0.9 %copy-start.3 = (f32[136,128]{1,0:T(8,128)S(1)}, f32[136,128]{1,0:T(8,128)}, u32[]{:S(2)}) copy-start(f32[136,128]{1,0:T(8,128)} %constant.17.clone.lag_hbm) | copy-start | bytes 208900
  4.5 0.8 %copy-start.4 = (bf16[128,256]{1,0:T(8,128)(2,1)S(1)}, bf16[128,256]{1,0:T(8,128)(2,1)}, u32[]{:S(2)}) copy-start(bf16[128,256]{1,0:T(8,128)(2,1)} %constant.16.clone.final_hbm) | copy-start | bytes 196612
  5.4 0.8 %copy-start.5 = (bf16[256,128]{1,0:T(8,128)(2,1)S(1)}, bf16[256,128]{1,0:T(8,128)(2,1)}, u32[]{:S(2)}) copy-start(bf16[256,128]{1,0:T(8,128)(2,1)} %constant.13.clone.left_hbm) | copy-start | bytes 196612
  6.2 0.8 %copy-start.6 = (bf16[128,128]{1,0:T(8,128)(2,1)S(1)}, bf16[128,128]{1,0:T(8,128)(2,1)}, u32[]{:S(2)}) copy-start(bf16[128,128]{1,0:T(8,128)(2,1)} %constant.12.clone.band_hbm) | copy-start | bytes 98308
  7.0 0.7 %copy-start.7 = (s32[1,4,128]{2,1,0:T(4,128)S(1)}, s32[1,4,128]{2,1,0:T(4,128)}, u32[]{:S(2)}) copy-start(s32[1,4,128]{2,1,0:T(4,128)} %links.1) | copy-start | bytes 6148
  7.7 0.7 %copy-start.8 = (s32[1,2,16]{2,1,0:T(2,128)S(1)}, s32[1,2,16]{2,1,0:T(2,128)}, u32[]{:S(2)}) copy-start(s32[1,2,16]{2,1,0:T(2,128)} %pair_slots.1) | copy-start | bytes 388
  8.3 0.7 %copy-start.9 = (s32[1,32]{1,0:T(1,128)S(1)}, s32[1,32]{1,0:T(1,128)}, u32[]{:S(2)}) copy-start(s32[1,32]{1,0:T(1,128)} %send_index.1) | copy-start | bytes 388

commit v2 on v1

--- a/solution.py
+++ b/solution.py
@@ -49,9 +49,9 @@
 def kernel(
     tile_count,
     mesh_count,
-    send_index,
-    pair_slots,
-    links,
+    send_hbm,
+    slots_hbm,
+    links_hbm,
     patches_hbm,
     band_hbm,
     left_hbm,
@@ -61,6 +61,9 @@
     lag_hbm,
     pair_out,
     relaxed_out,
+    send_index,
+    pair_slots,
+    links,
     patches,
     band,
     left,
@@ -92,6 +95,9 @@
         for n, (src, dst) in enumerate(
             (
                 (patches_hbm, patches),
+                (send_hbm, send_index),
+                (slots_hbm, pair_slots),
+                (links_hbm, links),
                 (band_hbm, band),
                 (left_hbm, left),
                 (right_hbm, right),
@@ -118,6 +124,7 @@
             barrier, inc=1, device_id={"mesh": lax.rem(lane + hop, mesh_count)}, device_id_type=MESH
         )
     fetch[0].wait()
+    fetch[1].wait()
 
     def picked(step, slot):
         index = send_index[0, other_of(me, step, tile_count) * capacity + slot]
@@ -139,21 +146,20 @@
         for slot in range(capacity):
             stage[step * capacity + slot] = picked(step, slot)
 
-    fill(tile_count - 1)
+    fill(1)
     pl.semaphore_wait(barrier, tile_count + mesh_count - 2)
-    sending(tile_count - 1).start()
-
-    def send(turn, carry):
-        step = tile_count - 1 - turn
+    sending(1).start()
+
+    def send(step, carry):
         fill(step)
         sending(step).start()
         return carry
 
-    lax.fori_loop(1, tile_count - 1, send, 0)
+    lax.fori_loop(2, tile_count, send, 0)
     for slot in range(capacity):
         recv[slot] = picked(0, slot)
 
-    for copy in fetch[1:]:
+    for copy in fetch[2:]:
         copy.wait()
 
     def prepare(step):
@@ -172,10 +178,8 @@
                 spectrum[step * capacity + first + n] = dot(both, right[...])
 
     prepare(0)
-    half = tile_count // 2
-
-    def take(turn, carry):
-        step = jnp.where(turn < half, turn, tile_count - 1 - (turn - half))
+
+    def take(step, carry):
         sending(step).wait_recv()
         prepare(step)
         return carry
@@ -185,34 +189,28 @@
     def place(slot):
         return other_of(me, slot // capacity, tile_count) * capacity + slot % capacity
 
-    group = 2 if pair_count % 2 == 0 else 1
-
-    def finish(turn, carry):
-        backs = []
-        lives = []
-        for n in range(group):
-            pair = turn * group + n
-            moving_slot = pair_slots[0, 0, pair]
-            fixed_slot = pair_slots[0, 1, pair]
-            live = jnp.logical_and(moving_slot < slot_total, fixed_slot < slot_total)
-            lives.append(jnp.where(live, 1.0, 0.0).astype(F32))
-            moving = spectrum[place(jnp.minimum(moving_slot, slot_total - 1))]
-            fixed = spectrum[place(jnp.minimum(fixed_slot, slot_total - 1))]
-            mr, mi = moving[:, :side], moving[:, side:]
-            fr, fi = fixed[:, :side], fixed[:, side:]
-            power = jnp.concatenate([mr * fr + mi * fi, mi * fr - mr * fi], 1).astype(BF16)
-            mixed = dot(power, back[...]).astype(BF16)
-            backs.append(jnp.concatenate([mixed[:, :side], mixed[:, side:]], 0))
-        surface = dot(final[...], jnp.concatenate(backs, 1))
-        weight = surface * surface
-        for n in range(group):
-            part = weight[:, n * side : (n + 1) * side]
-            pair = turn * group + n
-            sums[0, pl.ds(pair, 1), :] = lives[n] * jnp.sum(part, axis=0, keepdims=True)
-            sums[1, pl.ds(pair, 1), :] = lives[n] * jnp.sum(lag[:side] * part, axis=0, keepdims=True)
-        return carry
-
-    lax.fori_loop(0, pair_count // group, finish, 0)
+
+    backs = []
+    lives = []
+    for pair in range(pair_count):
+        moving_slot = pair_slots[0, 0, pair]
+        fixed_slot = pair_slots[0, 1, pair]
+        live = jnp.logical_and(moving_slot < slot_total, fixed_slot < slot_total)
+        lives.append(jnp.where(live, 1.0, 0.0).astype(F32))
+        moving = spectrum[place(jnp.minimum(moving_slot, slot_total - 1))]
+        fixed = spectrum[place(jnp.minimum(fixed_slot, slot_total - 1))]
+        mr, mi = moving[:, :side], moving[:, side:]
+        fr, fi = fixed[:, :side], fixed[:, side:]
+        power = jnp.concatenate([mr * fr + mi * fi, mi * fr - mr * fi], 1).astype(BF16)
+        mixed = dot(power, back[...]).astype(BF16)
+        backs.append(jnp.concatenate([mixed[:, :side], mixed[:, side:]], 0))
+    for pair in range(pair_count):
+        if pair % 2 == 0:
+            surface = dot(final[...], jnp.concatenate(backs[pair : pair + 2], 1))
+            weight = surface * surface
+        part = weight[:, pair % 2 * side : (pair % 2 + 1) * side]
+        sums[0, pair : pair + 1, :] = lives[pair] * jnp.sum(part, axis=0, keepdims=True)
+        sums[1, pair : pair + 1, :] = lives[pair] * jnp.sum(lag[:side] * part, axis=0, keepdims=True)
 
     scale = 1.0 / (side * side)
     total = sums[0]
@@ -280,10 +278,12 @@
     lags[:side] = lag[:, None]
     lags[side:] = lag[None, :]
     tables = [jnp.asarray(table) for table in (band, left, right, back, final, lags)]
-    smem = pl.BlockSpec(memory_space=pltpu.SMEM)
     vmem = pl.BlockSpec(memory_space=pltpu.VMEM)
-    hbm = pl.BlockSpec(memory_space=pl.ANY)
+    hbm = pl.BlockSpec(memory_space=pltpu.HBM)
     scratch = [
+        pltpu.SMEM(send_index.shape, jnp.int32),
+        pltpu.SMEM(pair_slots.shape, jnp.int32),
+        pltpu.VMEM(node_links.shape, jnp.int32),
         pltpu.VMEM(patches.shape, BF16),
         *[pltpu.VMEM(table.shape, table.dtype) for table in tables],
         pltpu.VMEM((slot_total, side, side), BF16),
@@ -291,7 +291,7 @@
         pltpu.VMEM((slot_total, side, 2 * side), F32),
         pltpu.VMEM((2, pair_count, side), F32),
         pltpu.VMEM((mesh_count, 2, pair_count, side), F32),
-        pltpu.SemaphoreType.DMA((1 + len(tables),)),
+        pltpu.SemaphoreType.DMA((4 + len(tables),)),
         pltpu.SemaphoreType.DMA((tile_count,)),
         pltpu.SemaphoreType.DMA((tile_count,)),
         pltpu.SemaphoreType.DMA((mesh_count,)),
@@ -303,11 +303,11 @@
             jax.ShapeDtypeStruct((2, pair_count), F32),
             jax.ShapeDtypeStruct((2, nodes), F32),
         ),
-        in_specs=[smem, smem, vmem, hbm] + [hbm] * len(tables),
+        in_specs=[hbm] * (4 + len(tables)),
         out_specs=(vmem, vmem),
         scratch_shapes=scratch,
         compiler_params=pltpu.CompilerParams(
-            collective_id=0, has_side_effects=True, vmem_limit_bytes=48 * 2**20
+            collective_id=0, has_side_effects=True, vmem_limit_bytes=60 * 2**20
         ),
         name="flow",
     )(send_index, pair_slots, node_links, patches, *tables)

time: 47.1 us -> 34.4 us (0.73)
  the two profiles are of different devices: /device:TPU:0 before, /device:TPU:11 now
where the time goes in v2:
time: 34.4 us; the launch traced here: 34.2 us
  Pallas kernels  31.7 us (92%)
  local copies, waits for them, and re-layouts  1.85 us (5%)
  between operations  0.65 us (2%)
    pallas_call x1, Pallas kernels, per_device(): pl.pallas_call(functools.partial(kernel, tile_count, mesh_count), out_sha...  31.7 us
    unnamed x6, local copies, waits for them, and re-layouts  1.85 us

profile of v2, /device:TPU:11, one launch (start us, length us, event | category | flops | bytes accessed | tf_op | source)
XLA Modules:
  0.0 34.2 jit_solution(15646773854973568883)
XLA Ops:
  0.6 31.7 %flow.1 = (f32[2,16]{1,0:T(2,128)}, f32[2,128]{1,0:T(2,128)}) custom-call(s32[1,32]{1,0:T(1,128)} %send_hbm.1, s32[1,2,16]{2,1,0:T(2,128)} %slots_hbm.1, s32[1,4,128]{2,1,0:T(4,128)} %links_hbm.1, bf16[32,128,128]{2,1,0:T(8,128)(2,1)} %patches_hbm.1, bf16[128,128]{1,0:T(8,128)(2,1)} %constant.12.clone.band_hbm, bf16[256,128]{1,0:T(8,128)(2,1)} %constant.13.clone.left_hbm, ...), custom_call_target="tpu_custom_call" | custom-call | tf_op jit(solution)/shard_map/flow/pallas_call | solution.py:300
  32.4 0.0 copy-start.1
  32.4 0.7 %copy-done.1 = f32[2,16]{1,0:T(2,128)S(1)} copy-done((f32[2,16]{1,0:T(2,128)S(1)}, f32[2,16]{1,0:T(2,128)}, u32[]{:S(2)}) %copy-start.1) | copy-done | bytes 152
  33.0 0.0 copy-start
  33.0 0.6 %copy.14 = f32[2,16]{1,0:T(2,128)} copy(f32[2,16]{1,0:T(2,128)S(1)} %copy-done.1) | data formatting | bytes 256
  33.6 0.1 copy-done
  33.7 0.6 %copy.15 = f32[2,128]{1,0:T(2,128)} copy(f32[2,128]{1,0:T(2,128)S(1)} %copy-done) | data formatting | bytes 2048
Async XLA Ops:
  32.4 0.7 %copy-start.1 = (f32[2,16]{1,0:T(2,128)S(1)}, f32[2,16]{1,0:T(2,128)}, u32[]{:S(2)}) copy-start(f32[2,16]{1,0:T(2,128)} %get-tuple-element.4) | copy-start | bytes 388
  33.0 0.6 %copy-start = (f32[2,128]{1,0:T(2,128)S(1)}, f32[2,128]{1,0:T(2,128)}, u32[]{:S(2)}) copy-start(f32[2,128]{1,0:T(2,128)} %get-tuple-element.5) | copy-start | bytes 3076

commit v3 on v2

--- a/solution.py
+++ b/solution.py
@@ -59,8 +59,7 @@
     back_hbm,
     final_hbm,
     lag_hbm,
-    pair_out,
-    relaxed_out,
+    out,
     send_index,
     pair_slots,
     links,
@@ -90,6 +89,20 @@
     capacity = slot_total // tile_count
     pair_count = pair_slots.shape[-1]
 
+    barrier = pltpu.get_barrier_semaphore()
+
+    def greet(turn, carry):
+        step = tile_count - turn
+        pl.semaphore_signal(
+            barrier, inc=1, device_id={"tiles": other_of(me, step, tile_count)}, device_id_type=MESH
+        )
+        return carry
+
+    lax.fori_loop(1, tile_count, greet, 0)
+    for hop in range(1, mesh_count):
+        pl.semaphore_signal(
+            barrier, inc=1, device_id={"mesh": lax.rem(lane + hop, mesh_count)}, device_id_type=MESH
+        )
     fetch = [
         pltpu.make_async_copy(src, dst, load_sem.at[n])
         for n, (src, dst) in enumerate(
@@ -110,19 +123,6 @@
     for copy in fetch:
         copy.start()
 
-    barrier = pltpu.get_barrier_semaphore()
-
-    def greet(step, carry):
-        pl.semaphore_signal(
-            barrier, inc=1, device_id={"tiles": other_of(me, step, tile_count)}, device_id_type=MESH
-        )
-        return carry
-
-    lax.fori_loop(1, tile_count, greet, 0)
-    for hop in range(1, mesh_count):
-        pl.semaphore_signal(
-            barrier, inc=1, device_id={"mesh": lax.rem(lane + hop, mesh_count)}, device_id_type=MESH
-        )
     fetch[0].wait()
     fetch[1].wait()
 
@@ -131,13 +131,16 @@
         block = patches[jnp.minimum(index, patch_count - 1)]
         return jnp.where(index < patch_count, block, jnp.zeros_like(block))
 
-    def sending(step):
-        block = pl.ds(step * capacity, capacity)
+    pieces = 2 if capacity % 2 == 0 else 1
+    piece = capacity // pieces
+
+    def sending(step, part):
+        block = pl.ds(step * capacity + part * piece, piece)
         return pltpu.make_async_remote_copy(
             src_ref=stage.at[block],
             dst_ref=recv.at[block],
-            send_sem=send_sem.at[step],
-            recv_sem=recv_sem.at[step],
+            send_sem=send_sem.at[step, part],
+            recv_sem=recv_sem.at[step, part],
             device_id={"tiles": other_of(me, step, tile_count)},
             device_id_type=MESH,
         )
@@ -148,11 +151,13 @@
 
     fill(1)
     pl.semaphore_wait(barrier, tile_count + mesh_count - 2)
-    sending(1).start()
+    for part in range(pieces):
+        sending(1, part).start()
 
     def send(step, carry):
         fill(step)
-        sending(step).start()
+        for part in range(pieces):
+            sending(step, part).start()
         return carry
 
     lax.fori_loop(2, tile_count, send, 0)
@@ -162,11 +167,11 @@
     for copy in fetch[2:]:
         copy.wait()
 
-    def prepare(step):
-        blocks = [recv[step * capacity + slot] for slot in range(capacity)]
-        width = 2 if capacity % 2 == 0 else 1
-        for first in range(0, capacity, width):
-            wide = jnp.concatenate(blocks[first : first + width], 1)
+    def prepare(step, part):
+        width = 2 if piece % 2 == 0 else 1
+        for first in range(part * piece, part * piece + piece, width):
+            blocks = [recv[step * capacity + first + n] for n in range(width)]
+            wide = jnp.concatenate(blocks, 1)
             partial = dot(band[...], wide).astype(BF16)
             tall = jnp.concatenate([partial[:, n * side : (n + 1) * side] for n in range(width)], 0)
             filtered = dot(tall, band[...]).astype(BF16)
@@ -177,11 +182,13 @@
                 both = jnp.concatenate([columns[:side], columns[side:]], 1)
                 spectrum[step * capacity + first + n] = dot(both, right[...])
 
-    prepare(0)
+    for part in range(pieces):
+        prepare(0, part)
 
     def take(step, carry):
-        sending(step).wait_recv()
-        prepare(step)
+        for part in range(pieces):
+            sending(step, part).wait_recv()
+            prepare(step, part)
         return carry
 
     lax.fori_loop(1, tile_count, take, 0)
@@ -237,7 +244,7 @@
     columns = lax.broadcasted_iota(jnp.int32, (pair_count, side), 1)
     for axis in range(2):
         line = jnp.sum(jnp.where(rows == columns, own[axis], 0.0), axis=0, keepdims=True)
-        pair_out[pl.ds(axis, 1), :] = line[:, :pair_count]
+        out[pl.ds(axis, 1), :] = line
 
     nodes = links.shape[-1]
     link_count = links.shape[1]
@@ -253,13 +260,19 @@
         for number in range(mesh_count):
             part = shares[number * pair_count : (number + 1) * pair_count]
             line = line + jnp.sum(part * flows[number, axis][:, :nodes], axis=0, keepdims=True)
-        relaxed_out[pl.ds(axis, 1), :] = line
+        out[pl.ds(2 + axis, 1), :] = line
 
     def drain(step, carry):
-        sending(step).wait_send()
+        for part in range(pieces):
+            sending(step, part).wait_send()
         return carry
 
     lax.fori_loop(1, tile_count, drain, 0)
+
+
+def split_outputs(both, pair_out, relaxed_out):
+    pair_out[...] = both[0:2, : pair_out.shape[1]]
+    relaxed_out[...] = both[2:4, :]
 
 
 def per_device(patches, send_index, pair_slots, node_links):
@@ -292,25 +305,32 @@
         pltpu.VMEM((2, pair_count, side), F32),
         pltpu.VMEM((mesh_count, 2, pair_count, side), F32),
         pltpu.SemaphoreType.DMA((4 + len(tables),)),
-        pltpu.SemaphoreType.DMA((tile_count,)),
-        pltpu.SemaphoreType.DMA((tile_count,)),
+        pltpu.SemaphoreType.DMA((tile_count, 2)),
+        pltpu.SemaphoreType.DMA((tile_count, 2)),
         pltpu.SemaphoreType.DMA((mesh_count,)),
         pltpu.SemaphoreType.DMA((mesh_count,)),
     ]
-    return pl.pallas_call(
+    both = pl.pallas_call(
         functools.partial(kernel, tile_count, mesh_count),
-        out_shape=(
-            jax.ShapeDtypeStruct((2, pair_count), F32),
-            jax.ShapeDtypeStruct((2, nodes), F32),
-        ),
+        out_shape=jax.ShapeDtypeStruct((4, nodes), F32),
         in_specs=[hbm] * (4 + len(tables)),
-        out_specs=(vmem, vmem),
+        out_specs=vmem,
         scratch_shapes=scratch,
         compiler_params=pltpu.CompilerParams(
             collective_id=0, has_side_effects=True, vmem_limit_bytes=60 * 2**20
         ),
         name="flow",
     )(send_index, pair_slots, node_links, patches, *tables)
+    return pl.pallas_call(
+        split_outputs,
+        out_shape=(
+            jax.ShapeDtypeStruct((2, pair_count), F32),
+            jax.ShapeDtypeStruct((2, nodes), F32),
+        ),
+        in_specs=[vmem],
+        out_specs=(vmem, vmem),
+        name="split",
+    )(both)
 
 
 def solution(mesh):

time: 34.4 us -> 33.8 us (0.983)
  the two profiles are of different devices: /device:TPU:11 before, /device:TPU:0 now
where the time goes in v3:
time: 33.8 us; the launch traced here: 33.5 us
  Pallas kernels  32.9 us (97%)
  between operations  0.64 us (2%)
    pallas_call x1, Pallas kernels, per_device(): pl.pallas_call(functools.partial(kernel, tile_count, mesh_count), out_sha...  31.7 us
    pallas_call x1, Pallas kernels, per_device(): pl.pallas_call(split_outputs, out_shape=(jax.ShapeDtypeStruct((2, pair_co...  1.25 us

profile of v3, /device:TPU:0, one launch (start us, length us, event | category | flops | bytes accessed | tf_op | source)
XLA Modules:
  0.0 33.5 jit_solution(4113453174718339233)
XLA Ops:
  0.6 31.7 %flow.1.both = f32[4,128]{1,0:T(4,128)} custom-call(s32[1,32]{1,0:T(1,128)} %send_hbm.1, s32[1,2,16]{2,1,0:T(2,128)} %slots_hbm.1, s32[1,4,128]{2,1,0:T(4,128)} %links_hbm.1, bf16[32,128,128]{2,1,0:T(8,128)(2,1)} %patches_hbm.1, bf16[128,128]{1,0:T(8,128)(2,1)} %constant.12.clone.band_hbm, bf16[256,128]{1,0:T(8,128)(2,1)} %constant.13.clone.left_hbm, ...), custom_call_target="tpu_custom_call" | custom-call | tf_op jit(solution)/shard_map/flow/pallas_call | solution.py:313
  32.3 1.3 %split.1 = (f32[2,16]{1,0:T(2,128)}, f32[2,128]{1,0:T(2,128)}) custom-call(f32[4,128]{1,0:T(4,128)} %flow.1.both), custom_call_target="tpu_custom_call" | custom-call | tf_op jit(solution)/shard_map/split/pallas_call | solution.py:324

commit v4 on v3

--- a/solution.py
+++ b/solution.py
@@ -199,6 +199,15 @@
 
     backs = []
     lives = []
+
+    def settle(first):
+        surface = dot(final[...], jnp.concatenate(backs[first : first + 2], 1))
+        weight = surface * surface
+        for pair in range(first, min(first + 2, pair_count)):
+            part = weight[:, pair % 2 * side : (pair % 2 + 1) * side]
+            sums[0, pair : pair + 1, :] = lives[pair] * jnp.sum(part, axis=0, keepdims=True)
+            sums[1, pair : pair + 1, :] = lives[pair] * jnp.sum(lag[:side] * part, axis=0, keepdims=True)
+
     for pair in range(pair_count):
         moving_slot = pair_slots[0, 0, pair]
         fixed_slot = pair_slots[0, 1, pair]
@@ -211,13 +220,10 @@
         power = jnp.concatenate([mr * fr + mi * fi, mi * fr - mr * fi], 1).astype(BF16)
         mixed = dot(power, back[...]).astype(BF16)
         backs.append(jnp.concatenate([mixed[:, :side], mixed[:, side:]], 0))
-    for pair in range(pair_count):
-        if pair % 2 == 0:
-            surface = dot(final[...], jnp.concatenate(backs[pair : pair + 2], 1))
-            weight = surface * surface
-        part = weight[:, pair % 2 * side : (pair % 2 + 1) * side]
-        sums[0, pair : pair + 1, :] = lives[pair] * jnp.sum(part, axis=0, keepdims=True)
-        sums[1, pair : pair + 1, :] = lives[pair] * jnp.sum(lag[:side] * part, axis=0, keepdims=True)
+        if pair % 2 == 1 and pair >= 5:
+            settle(pair - 5)
+    for first in range(max(0, pair_count - 4 - pair_count % 2), pair_count, 2):
+        settle(first)
 
     scale = 1.0 / (side * side)
     total = sums[0]

time: 33.8 us -> 33.9 us (level)
  no operation moved by 1% of the time
where the time goes in v4:
time: 33.9 us; the launch traced here: 33.7 us
  Pallas kernels  33 us (97%)
  between operations  0.64 us (2%)
    pallas_call x1, Pallas kernels, per_device(): pl.pallas_call(functools.partial(kernel, tile_count, mesh_count), out_sha...  31.8 us
    pallas_call x1, Pallas kernels, per_device(): pl.pallas_call(split_outputs, out_shape=(jax.ShapeDtypeStruct((2, pair_co...  1.25 us

profile of v4, /device:TPU:0, one launch (start us, length us, event | category | flops | bytes accessed | tf_op | source)
XLA Modules:
  0.0 33.7 jit_solution(14619767286888030948)
XLA Ops:
  0.6 31.8 %flow.1.both = f32[4,128]{1,0:T(4,128)} custom-call(s32[1,32]{1,0:T(1,128)} %send_hbm.1, s32[1,2,16]{2,1,0:T(2,128)} %slots_hbm.1, s32[1,4,128]{2,1,0:T(4,128)} %links_hbm.1, bf16[32,128,128]{2,1,0:T(8,128)(2,1)} %patches_hbm.1, bf16[128,128]{1,0:T(8,128)(2,1)} %constant.12.clone.band_hbm, bf16[256,128]{1,0:T(8,128)(2,1)} %constant.13.clone.left_hbm, ...), custom_call_target="tpu_custom_call" | custom-call | tf_op jit(solution)/shard_map/flow/pallas_call | solution.py:319
  32.4 1.3 %split.1 = (f32[2,16]{1,0:T(2,128)}, f32[2,128]{1,0:T(2,128)}) custom-call(f32[4,128]{1,0:T(4,128)} %flow.1.both), custom_call_target="tpu_custom_call" | custom-call | tf_op jit(solution)/shard_map/split/pallas_call | solution.py:330
